TPU v7x, 32 devices: a whole 2x2x4 slice. The times are simulated.
32 devices in a mesh: dp: 8 (over z, x), mp: 4 (over y, core).
Axes of the slice: x: 2, y: 2, z: 4, core: 2. Of those that a mesh axis runs over, the one named last changes fastest.
Arguments:
- tokens: bfloat16 [8, 1024, 1024], P('dp', 'mp'), may hold values from -6 to 6
- seg_lengths: int32 [8, 2], P('dp'), may hold values from 1 to 896, 1024 in all within a row
- cotangent: bfloat16 [8, 1024, 1024], P('dp', 'mp'), may hold values from -6 to 6
- mixer_norm_gain: float32 [2, 1024], replicated, may hold values from 0.5 to 1.5
- mixer_norm_bias: float32 [2, 1024], replicated, may hold values from -3 to 3
- in_weight: bfloat16 [2, 1024, 3, 1024], P(None, None, None, 'mp'), may hold values from -0.1875 to 0.1875
- in_bias: float32 [2, 3, 1024], P(None, None, 'mp'), may hold values from -3 to 3
- conv_weight: float32 [2, 3, 3, 1024], P(None, None, None, 'mp'), may hold values from -3 to 3
- conv_bias: float32 [2, 3, 1024], P(None, None, 'mp'), may hold values from -3 to 3
- filter_in: float32 [2, 33, 64], replicated, may hold values from -1 to 1
- filter_in_bias: float32 [2, 64], replicated, may hold values from -4 to 4
- filter_in_freq: float32 [2, 64], replicated, may hold values from 0.1 to 1.9
- filter_mid: float32 [2, 64, 64], replicated, may hold values from -0.75 to 0.75
- filter_mid_bias: float32 [2, 64], replicated, may hold values from -4 to 4
- filter_mid_freq: float32 [2, 64], replicated, may hold values from 0.1 to 1.9
- filter_out: float32 [2, 64, 1024], P(None, None, 'mp'), may hold values from -0.09375 to 0.09375
- skip_bias: float32 [2, 1024], P(None, 'mp'), may hold values from -4 to 4
- out_weight: bfloat16 [2, 1024, 1024], P(None, 'mp'), may hold values from -0.1875 to 0.1875
- out_bias: float32 [2, 1024], replicated, may hold values from -3 to 3
- feed_norm_gain: float32 [2, 1024], replicated, may hold values from 0.5 to 1.5
- feed_norm_bias: float32 [2, 1024], replicated, may hold values from -3 to 3
- feed_up: bfloat16 [2, 1024, 4096], P(None, None, 'mp'), may hold values from -0.1875 to 0.1875
- feed_up_bias: float32 [2, 4096], P(None, 'mp'), may hold values from -3 to 3
- feed_down: bfloat16 [2, 4096, 1024], P(None, 'mp'), may hold values from -0.09375 to 0.09375
- feed_down_bias: float32 [2, 1024], replicated, may hold values from -3 to 3
Outputs:
- outputs: float32 [8, 1024, 1024], P('dp', 'mp')
- token_grad: float32 [8, 1024, 1024], P('dp', 'mp')
- mixer_norm_gain_grad: float32 [2, 1024], replicated
- mixer_norm_bias_grad: float32 [2, 1024], replicated
- in_weight_grad: float32 [2, 1024, 3, 1024], P(None, 'dp', None, 'mp')
- in_bias_grad: float32 [2, 3, 1024], P(None, None, 'mp')
- conv_weight_grad: float32 [2, 3, 3, 1024], P(None, None, None, 'mp')
- conv_bias_grad: float32 [2, 3, 1024], P(None, None, 'mp')
- filter_in_grad: float32 [2, 33, 64], replicated
- filter_in_bias_grad: float32 [2, 64], replicated
- filter_in_freq_grad: float32 [2, 64], replicated
- filter_mid_grad: float32 [2, 64, 64], replicated
- filter_mid_bias_grad: float32 [2, 64], replicated
- filter_mid_freq_grad: float32 [2, 64], replicated
- filter_out_grad: float32 [2, 64, 1024], P(None, None, 'mp')
- skip_bias_grad: float32 [2, 1024], P(None, 'mp')
- out_weight_grad: float32 [2, 1024, 1024], P(None, 'mp', 'dp')
- out_bias_grad: float32 [2, 1024], replicated
- feed_norm_gain_grad: float32 [2, 1024], replicated
- feed_norm_bias_grad: float32 [2, 1024], replicated
- feed_up_grad: float32 [2, 1024, 4096], P(None, 'dp', 'mp')
- feed_up_bias_grad: float32 [2, 4096], P(None, 'mp')
- feed_down_grad: float32 [2, 4096, 1024], P(None, 'mp', 'dp')
- feed_down_bias_grad: float32 [2, 1024], replicated
Inputs may be any that keep to these rules, and one draw needn't show every extreme that they name: `seg_lengths`: each row's 2 segment lengths sum to 1024; none is longer than 896.
All inputs are finite; a program needn't handle non-finite values.
Results may differ from a plain program's by a relative error of at most 0.023.
Values may be sent and summed in bfloat16 or wider, within the bound.
No kernel may reach another device: no remote copies, remote signals or barrier semaphores. Data moves between devices by JAX's collectives and lax.ppermute only.
A program may use at most 256 MiB of HBM per device.

v0:
```python
import math

import jax
import jax.numpy as jnp
from jax import lax
from jax.sharding import PartitionSpec as P

D = 1024
POS = 33


highest = lax.Precision.HIGHEST
norm_eps = 1e-05
slow_rate = math.log(100.0) / 1.5
fast_rate = math.log(100.0) / 0.3


def segment_tables(lengths, length):
    seg_ends = jnp.cumsum(lengths)
    starts = seg_ends - lengths
    places = jnp.arange(length, dtype=jnp.int32)
    inside = (places[None, :] >= starts[:, None]) & (places[None, :] < seg_ends[:, None])
    seg_masks = inside.astype(jnp.float32)
    seg_offset = jnp.sum(jnp.where(inside, places[None, :] - starts[:, None], 0), axis=0)
    return (seg_masks, seg_offset)


def position_table(length):
    places = jnp.arange(length, dtype=jnp.int32).astype(jnp.float32)
    band_count = (POS - 1) // 2
    band_index = jnp.arange(band_count, dtype=jnp.int32).astype(jnp.float32)
    band_freq = 0.0001 + band_index * ((band_count - 1 - 0.0001) / (band_count - 1))
    phases = places[:, None] * band_freq[None, :] * (2.0 * math.pi / length)
    return jnp.concatenate(
        [places[:, None] / (length - 1), jnp.cos(phases), -jnp.sin(phases)], axis=1
    )


def decay_window(length, chan_index):
    places = jnp.arange(length, dtype=jnp.int32).astype(jnp.float32)
    decay_rates = slow_rate + (fast_rate - slow_rate) * chan_index / (D - 1)
    return jnp.exp(-(places[:, None] / (length - 1)) * decay_rates[None, :])


def make_taps(
    filter_in,
    filter_in_bias,
    filter_in_freq,
    filter_mid,
    filter_mid_bias,
    filter_mid_freq,
    filter_out,
    pos_table,
):
    hidden = jnp.sin(
        filter_in_freq * (jnp.dot(pos_table, filter_in, precision=highest) + filter_in_bias)
    )
    hidden = jnp.sin(
        filter_mid_freq * (jnp.dot(hidden, filter_mid, precision=highest) + filter_mid_bias)
    )
    return jnp.dot(hidden, filter_out, precision=highest)


def layer_norm(values, gain_row, shift_row):
    center = values - jnp.mean(values, axis=-1, keepdims=True)
    spread = jnp.mean(center * center, axis=-1, keepdims=True)
    return center * lax.rsqrt(spread + norm_eps) * gain_row + shift_row


def short_conv(proj_in, conv_weight, seg_offset):
    summed = proj_in * conv_weight[:, 0]
    for lag_index in range(1, conv_weight.shape[1]):
        shifted = jnp.pad(proj_in[:-lag_index], ((lag_index, 0), (0, 0), (0, 0)))
        kept_mask = (seg_offset >= lag_index).astype(jnp.float32)
        summed = summed + shifted * conv_weight[:, lag_index] * kept_mask[:, None, None]
    return summed


def dft_plan(length):
    dft_size = 2 * length
    inner = 1
    while inner * inner * 4 <= dft_size:
        inner = inner * 2
    return (dft_size, inner, dft_size // inner)


def trig_table(row_count, col_count, dft_size):
    product = (
        jnp.arange(row_count, dtype=jnp.int32)[:, None]
        * jnp.arange(col_count, dtype=jnp.int32)[None, :]
        % dft_size
    )
    phases = product.astype(jnp.float32) * (2.0 * math.pi / dft_size)
    return (jnp.cos(phases), jnp.sin(phases))


def forward_dft(signal, length):
    dft_size, inner, outer = dft_plan(length)
    blocks = signal.reshape(signal.shape[0], outer // 2, inner, signal.shape[-1])
    outer_cos, outer_sin = trig_table(outer // 2, outer, outer)
    twist_cos, twist_sin = trig_table(outer, inner, dft_size)
    twist_cos = twist_cos[None, :, :, None]
    twist_sin = twist_sin[None, :, :, None]
    inner_cos, inner_sin = trig_table(inner, inner, inner)
    first_re = jnp.einsum("bnpc,nk->bkpc", blocks, outer_cos, precision=highest)
    first_im = -jnp.einsum("bnpc,nk->bkpc", blocks, outer_sin, precision=highest)
    twist_re = first_re * twist_cos + first_im * twist_sin
    twist_im = first_im * twist_cos - first_re * twist_sin
    spec_re = jnp.einsum("bkpc,pq->bkqc", twist_re, inner_cos, precision=highest) + jnp.einsum(
        "bkpc,pq->bkqc", twist_im, inner_sin, precision=highest
    )
    spec_im = jnp.einsum("bkpc,pq->bkqc", twist_im, inner_cos, precision=highest) - jnp.einsum(
        "bkpc,pq->bkqc", twist_re, inner_sin, precision=highest
    )
    return (spec_re, spec_im)


def inverse_dft(spec_re, spec_im, length):
    dft_size, inner, outer = dft_plan(length)
    outer_cos, outer_sin = trig_table(outer // 2, outer, outer)
    twist_cos, twist_sin = trig_table(outer, inner, dft_size)
    twist_cos = twist_cos[None, :, :, None]
    twist_sin = twist_sin[None, :, :, None]
    inner_cos, inner_sin = trig_table(inner, inner, inner)
    back_re = jnp.einsum("bkqc,pq->bkpc", spec_re, inner_cos, precision=highest) - jnp.einsum(
        "bkqc,pq->bkpc", spec_im, inner_sin, precision=highest
    )
    back_im = jnp.einsum("bkqc,pq->bkpc", spec_re, inner_sin, precision=highest) + jnp.einsum(
        "bkqc,pq->bkpc", spec_im, inner_cos, precision=highest
    )
    turn_re = back_re * twist_cos - back_im * twist_sin
    turn_im = back_re * twist_sin + back_im * twist_cos
    result = jnp.einsum("bkpc,nk->bnpc", turn_re, outer_cos, precision=highest) - jnp.einsum(
        "bkpc,nk->bnpc", turn_im, outer_sin, precision=highest
    )
    return result.reshape(spec_re.shape[0], length, spec_re.shape[-1]) / dft_size


def long_conv(values, filter_taps, seg_masks):
    length = values.shape[0]
    pieces = seg_masks[:, :, None] * values[None]
    taps_re, taps_im = forward_dft(filter_taps[None], length)
    piece_re, piece_im = forward_dft(pieces, length)
    prod_re = piece_re * taps_re - piece_im * taps_im
    prod_im = piece_re * taps_im + piece_im * taps_re
    results = inverse_dft(prod_re, prod_im, length)
    return jnp.sum(seg_masks[:, :, None] * results, axis=0)


def mixer(
    proj_in,
    conv_weight,
    conv_bias,
    filter_in,
    filter_in_bias,
    filter_in_freq,
    filter_mid,
    filter_mid_bias,
    filter_mid_freq,
    filter_out,
    skip_bias,
    pos_table,
    window,
    seg_masks,
    seg_offset,
):
    shorted = short_conv(proj_in, conv_weight, seg_offset) + conv_bias
    filter_taps = (
        make_taps(
            filter_in,
            filter_in_bias,
            filter_in_freq,
            filter_mid,
            filter_mid_bias,
            filter_mid_freq,
            filter_out,
            pos_table,
        )
        * window
    )
    gated = shorted[:, 2] * shorted[:, 1]
    longc = long_conv(gated, filter_taps, seg_masks) + skip_bias * gated
    return longc * shorted[:, 0]


def contract_rows(left, right):
    return lax.dot_general(
        left, right, (((0,), (0,)), ((), ())), preferred_element_type=jnp.float32
    )


def contract_cols(left, right):
    return lax.dot_general(
        left, right, (((1,), (1,)), ((), ())), preferred_element_type=jnp.float32
    )


def gather_rows(normed):
    return lax.all_gather(normed.astype(jnp.bfloat16), "mp", axis=0, tiled=True)


def scatter_rows(term_fn, local_rows):
    return lax.psum_scatter(
        term_fn(jnp.int32(0), local_rows * lax.axis_size("mp")).astype(jnp.bfloat16),
        "mp",
        scatter_dimension=0,
        tiled=True,
    ).astype(jnp.float32)


def gather_grads(gradient_low):
    return lax.all_gather(gradient_low, "mp", axis=0, tiled=True)


def scatter_grads(term_fn, local_rows):
    return lax.psum_scatter(
        term_fn(jnp.int32(0), local_rows * lax.axis_size("mp")).astype(jnp.bfloat16),
        "mp",
        scatter_dimension=0,
        tiled=True,
    ).astype(jnp.float32)


def shards(
    tokens,
    seg_lengths,
    cotangent,
    mixer_norm_gain,
    mixer_norm_bias,
    in_weight,
    in_bias,
    conv_weight,
    conv_bias,
    filter_in,
    filter_in_bias,
    filter_in_freq,
    filter_mid,
    filter_mid_bias,
    filter_mid_freq,
    filter_out,
    skip_bias,
    out_weight,
    out_bias,
    feed_norm_gain,
    feed_norm_bias,
    feed_up,
    feed_up_bias,
    feed_down,
    feed_down_bias,
):
    local_rows = tokens.shape[1]
    length = local_rows * lax.axis_size("mp")
    channels = in_weight.shape[3]
    layer_count = in_weight.shape[0]
    seg_masks, seg_offset = segment_tables(seg_lengths[0], length)
    chan_index = (lax.axis_index("mp") * channels + jnp.arange(channels, dtype=jnp.int32)).astype(
        jnp.float32
    )
    pos_table = position_table(length)
    window = decay_window(length, chan_index)

    def mixer_here(*mixer_args):
        return mixer(*mixer_args, pos_table, window, seg_masks, seg_offset)

    def layer_params(layer_index):
        return (
            conv_weight[layer_index],
            conv_bias[layer_index],
            filter_in[layer_index],
            filter_in_bias[layer_index],
            filter_in_freq[layer_index],
            filter_mid[layer_index],
            filter_mid_bias[layer_index],
            filter_mid_freq[layer_index],
            filter_out[layer_index],
            skip_bias[layer_index],
        )

    residual = tokens[0].astype(jnp.float32)
    stored = []
    for layer_index in range(layer_count):
        normed_rows = gather_rows(
            layer_norm(residual, mixer_norm_gain[layer_index], mixer_norm_bias[layer_index])
        )
        proj_in = (
            jnp.einsum(
                "td,dkc->tkc",
                normed_rows,
                in_weight[layer_index],
                preferred_element_type=jnp.float32,
            )
            + in_bias[layer_index]
        )
        mixed_low = mixer_here(proj_in, *layer_params(layer_index)).astype(jnp.bfloat16)
        branch = scatter_rows(
            lambda offset, amount, source=mixed_low, matrix=out_weight[layer_index]: jnp.dot(
                source, matrix, preferred_element_type=jnp.float32
            ),
            local_rows,
        )
        middle = residual + branch + out_bias[layer_index]
        feed_rows = gather_rows(
            layer_norm(middle, feed_norm_gain[layer_index], feed_norm_bias[layer_index])
        )
        preact = (
            jnp.dot(feed_rows, feed_up[layer_index], preferred_element_type=jnp.float32)
            + feed_up_bias[layer_index]
        )
        hidden = jax.nn.gelu(preact, approximate=True).astype(jnp.bfloat16)
        branch = scatter_rows(
            lambda offset, amount, source=hidden, matrix=feed_down[layer_index]: jnp.dot(
                source, matrix, preferred_element_type=jnp.float32
            ),
            local_rows,
        )
        stored.append(
            (residual, normed_rows, proj_in, mixed_low, middle, feed_rows, preact, hidden)
        )
        residual = middle + branch + feed_down_bias[layer_index]
    gradient = cotangent[0].astype(jnp.float32)
    shard_grads = [None] * layer_count
    shared_grads = [None] * layer_count
    for layer_index in reversed(range(layer_count)):
        residual_in, normed_rows, proj_in, mixed_low, middle, feed_rows, preact, hidden = stored[
            layer_index
        ]
        down_bias_grad = jnp.sum(gradient, axis=0)
        down_rows = gather_grads(gradient.astype(jnp.bfloat16))
        down_grad = contract_rows(hidden, down_rows)
        hidden_grad = contract_cols(down_rows, feed_down[layer_index])
        unused_gelu, gelu_pull = jax.vjp(
            lambda preact_in: jax.nn.gelu(preact_in, approximate=True), preact
        )
        pre_grad = gelu_pull(hidden_grad)[0]
        up_bias_grad = jnp.sum(pre_grad, axis=0)
        pre_low = pre_grad.astype(jnp.bfloat16)
        up_grad = contract_rows(feed_rows, pre_low)
        feed_normed_grad = scatter_grads(
            lambda offset, amount, source=pre_low, matrix=feed_up[layer_index]: contract_cols(
                source, matrix
            ),
            local_rows,
        )
        unused_norm, norm_pull = jax.vjp(
            layer_norm, middle, feed_norm_gain[layer_index], feed_norm_bias[layer_index]
        )
        middle_grad, feed_gain_grad, feed_shift_grad = norm_pull(feed_normed_grad)
        gradient = gradient + middle_grad
        out_bias_grad = jnp.sum(gradient, axis=0)
        out_rows = gather_grads(gradient.astype(jnp.bfloat16))
        out_grad = contract_rows(mixed_low, out_rows)
        mixed_grad = contract_cols(out_rows, out_weight[layer_index])
        unused_mixed, mixer_pull = jax.vjp(mixer_here, proj_in, *layer_params(layer_index))
        mixer_grads = mixer_pull(mixed_grad)
        proj_grad = mixer_grads[0]
        in_bias_grad = jnp.sum(proj_grad, axis=0)
        proj_low = proj_grad.astype(jnp.bfloat16)
        in_grad = jnp.einsum(
            "td,tkc->dkc", normed_rows, proj_low, preferred_element_type=jnp.float32
        )
        normed_grad = scatter_grads(
            lambda offset, amount, source=proj_low, matrix=in_weight[layer_index]: jnp.einsum(
                "tkc,dkc->td", source, matrix, preferred_element_type=jnp.float32
            ),
            local_rows,
        )
        unused_first, first_pull = jax.vjp(
            layer_norm, residual_in, mixer_norm_gain[layer_index], mixer_norm_bias[layer_index]
        )
        residual_grad, mixer_gain_grad, mixer_shift_grad = first_pull(normed_grad)
        gradient = gradient + residual_grad
        shard_grads[layer_index] = (
            in_grad,
            in_bias_grad,
            mixer_grads[1],
            mixer_grads[2],
            mixer_grads[9],
            mixer_grads[10],
            out_grad,
            up_grad,
            up_bias_grad,
            down_grad,
        )
        shared_grads[layer_index] = (
            mixer_gain_grad,
            mixer_shift_grad,
            mixer_grads[3],
            mixer_grads[4],
            mixer_grads[5],
            mixer_grads[6],
            mixer_grads[7],
            mixer_grads[8],
            out_bias_grad,
            feed_gain_grad,
            feed_shift_grad,
            down_bias_grad,
        )

    def stacked(kind):
        return jnp.stack([shard_grads[layer_index][kind] for layer_index in range(layer_count)])

    big = (
        lax.psum_scatter(stacked(0), "dp", scatter_dimension=1, tiled=True),
        lax.psum_scatter(stacked(6), "dp", scatter_dimension=2, tiled=True),
        lax.psum_scatter(stacked(7), "dp", scatter_dimension=1, tiled=True),
        lax.psum_scatter(stacked(9), "dp", scatter_dimension=2, tiled=True),
    )
    small = lax.psum((stacked(1), stacked(2), stacked(3), stacked(4), stacked(5), stacked(8)), "dp")
    stacks = [
        jnp.stack([shared_grads[layer_index][kind] for layer_index in range(layer_count)])
        for kind in range(12)
    ]
    shared = lax.psum(
        (
            stacks[0],
            stacks[1],
            stacks[2],
            stacks[3],
            stacks[4],
            stacks[5],
            stacks[6],
            stacks[7],
            stacks[8],
            stacks[9],
            stacks[10],
            stacks[11],
        ),
        ("dp", "mp"),
    )
    return (
        residual[None],
        gradient[None],
        shared[0],
        shared[1],
        big[0],
        small[0],
        small[1],
        small[2],
        shared[2],
        shared[3],
        shared[4],
        shared[5],
        shared[6],
        shared[7],
        small[3],
        small[4],
        big[1],
        shared[8],
        shared[9],
        shared[10],
        big[2],
        small[5],
        big[3],
        shared[11],
    )


def solution(mesh):
    in_specs = (
        P("dp", "mp", None),
        P("dp", None),
        P("dp", "mp", None),
        P(),
        P(),
        P(None, None, None, "mp"),
        P(None, None, "mp"),
        P(None, None, None, "mp"),
        P(None, None, "mp"),
        P(),
        P(),
        P(),
        P(),
        P(),
        P(),
        P(None, None, "mp"),
        P(None, "mp"),
        P(None, "mp", None),
        P(),
        P(),
        P(),
        P(None, None, "mp"),
        P(None, "mp"),
        P(None, "mp", None),
        P(),
    )
    out_specs = (
        P("dp", "mp", None),
        P("dp", "mp", None),
        P(),
        P(),
        P(None, "dp", None, "mp"),
        P(None, None, "mp"),
        P(None, None, None, "mp"),
        P(None, None, "mp"),
        P(),
        P(),
        P(),
        P(),
        P(),
        P(),
        P(None, None, "mp"),
        P(None, "mp"),
        P(None, "mp", "dp"),
        P(),
        P(),
        P(),
        P(None, "dp", "mp"),
        P(None, "mp"),
        P(None, "mp", "dp"),
        P(),
    )
    return jax.shard_map(shards, mesh=mesh, in_specs=in_specs, out_specs=out_specs, check_vma=False)
```

profile of v0, /device:TPU:0, one launch (start us, length us, event | category | flops | bytes accessed | tf_op | source)
XLA Modules:
  0.0 1669.9 jit_solution(5935750721067539322)
XLA Ops:
  51.0 14.9 fusion.250
  145.6 34.1 %reduce-scatter.13.cloned.1.call-done = bf16[256,1024]{1,0:T(8,128)(2,1)} async-done(((bf16[1024,1024]{1,0:T(8,128)(2,1)}), bf16[256,1024]{1,0:T(8,128)(2,1)}) %reduce-scatter.13.cloned.1.call-update) | async-done | bytes 524304 | tf_op jit(solution)/shard_map/reduce_scatter | solution.py:203
  184.7 22.7 %all-gather.12.cloned.1.call-done = bf16[1024,1024]{1,0:T(8,128)(2,1)} async-done(((bf16[256,1024]{1,0:T(8,128)(2,1)}), bf16[1024,1024]{1,0:T(8,128)(2,1)}) %all-gather.12.cloned.1.call-update) | async-done | bytes 2097168 | tf_op jit(solution)/shard_map/all_gather | solution.py:199
  218.3 31.5 %reduce-scatter.15.cloned.1.call-done = bf16[256,1024]{1,0:T(8,128)(2,1)} async-done(((bf16[1024,1024]{1,0:T(8,128)(2,1)}), bf16[256,1024]{1,0:T(8,128)(2,1)}) %reduce-scatter.15.cloned.1.call-update) | async-done | bytes 524304 | tf_op jit(solution)/shard_map/reduce_scatter | solution.py:203
  356.1 31.5 %reduce-scatter.17.cloned.1.call-done = bf16[256,1024]{1,0:T(8,128)(2,1)} async-done(((bf16[1024,1024]{1,0:T(8,128)(2,1)}), bf16[256,1024]{1,0:T(8,128)(2,1)}) %reduce-scatter.17.cloned.1.call-update) | async-done | bytes 524304 | tf_op jit(solution)/shard_map/reduce_scatter | solution.py:203
  391.9 21.8 %all-gather.16.cloned.1.call-done = bf16[1024,1024]{1,0:T(8,128)(2,1)} async-done(((bf16[256,1024]{1,0:T(8,128)(2,1)}), bf16[1024,1024]{1,0:T(8,128)(2,1)}) %all-gather.16.cloned.1.call-update) | async-done | bytes 2097168 | tf_op jit(solution)/shard_map/all_gather | solution.py:199
  420.2 17.7 %all-gather.24.cloned.1.call-done = bf16[1,1024,1024]{2,1,0:T(8,128)(2,1)} async-done(((bf16[1,256,1024]{2,1,0:T(8,128)(2,1)}), bf16[1,1024,1024]{2,1,0:T(8,128)(2,1)}) %all-gather.24.cloned.1.call-update) | async-done | bytes 2097168 | tf_op jit(solution)/shard_map/all_gather | solution.py:212
  437.9 9.0 fusion.972
  459.1 24.4 %reduce-scatter.21.cloned.1.call-done = bf16[256,1024]{1,0:T(8,128)(2,1)} async-done(((bf16[1024,1024]{1,0:T(8,128)(2,1)}), bf16[256,1024]{1,0:T(8,128)(2,1)}) %reduce-scatter.21.cloned.1.call-update) | async-done | bytes 524304 | tf_op jit(solution)/shard_map/reduce_scatter | solution.py:216
  485.3 32.0 %reduce-scatter.19.cloned.1.call-done = bf16[256,1024]{1,0:T(8,128)(2,1)} async-done(((bf16[1024,1024]{1,0:T(8,128)(2,1)}), bf16[256,1024]{1,0:T(8,128)(2,1)}) %reduce-scatter.19.cloned.1.call-update) | async-done | bytes 524304 | tf_op jit(solution)/shard_map/reduce_scatter | solution.py:203
  522.8 22.3 %all-gather.18.cloned.1.call-done = bf16[1024,1024]{1,0:T(8,128)(2,1)} async-done(((bf16[256,1024]{1,0:T(8,128)(2,1)}), bf16[1024,1024]{1,0:T(8,128)(2,1)}) %all-gather.18.cloned.1.call-update) | async-done | bytes 2097168 | tf_op jit(solution)/shard_map/all_gather | solution.py:212
  581.7 21.0 %fusion.14 = (f32[64,32,256]{2,1,0:T(8,128)}, f32[64,32,256]{2,1,0:T(8,128)}, f32[64,32,256]{2,1,0:T(8,128)}, f32[64,32,256]{2,1,0:T(8,128)}, f32[2,64,256,32]{2,3,1,0:T(8,128)}) fusion(f32[32,2,64,256]{3,0,2,1:T(8,128)} %copy-done.10, f32[2,64,256,32]{2,3,1,0:T(8,128)S(1)} %fusion.108, f32[32,2,64,256]{3,0,2,1:T(8,128)} %copy-done.9, ...), kind=kOutput, calls=%fused_computation.23 | convolution fusion | flops 411056128 | bytes 33554432 | tf_op jit(solution)/shard_map/transpose(jvp(bkqc,pq->bkpc))/dot_general | solution.py:128
  651.0 31.5 %reduce-scatter.23.cloned.1.call-done = bf16[256,1024]{1,0:T(8,128)(2,1)} async-done(((bf16[1024,1024]{1,0:T(8,128)(2,1)}), bf16[256,1024]{1,0:T(8,128)(2,1)}) %reduce-scatter.23.cloned.1.call-update) | async-done | bytes 524304 | tf_op jit(solution)/shard_map/reduce_scatter | solution.py:216
  689.1 22.7 %all-gather.20.cloned.1.call-done = bf16[1024,1024]{1,0:T(8,128)(2,1)} async-done(((bf16[256,1024]{1,0:T(8,128)(2,1)}), bf16[1024,1024]{1,0:T(8,128)(2,1)}) %all-gather.20.cloned.1.call-update) | async-done | bytes 2097168 | tf_op jit(solution)/shard_map/all_gather | solution.py:212
  711.8 9.0 fusion.973
  725.9 31.5 %reduce-scatter.25.cloned.1.call-done = bf16[256,1024]{1,0:T(8,128)(2,1)} async-done(((bf16[1024,1024]{1,0:T(8,128)(2,1)}), bf16[256,1024]{1,0:T(8,128)(2,1)}) %reduce-scatter.25.cloned.1.call-update) | async-done | bytes 524304 | tf_op jit(solution)/shard_map/reduce_scatter | solution.py:216
  822.8 18.7 %fusion.19 = (f32[64,32,256]{2,1,0:T(8,128)}, f32[64,32,256]{2,1,0:T(8,128)}, f32[64,32,256]{2,1,0:T(8,128)}, f32[64,32,256]{2,1,0:T(8,128)}, f32[2,64,256,32]{2,3,1,0:T(8,128)S(1)}) fusion(f32[32,2,64,256]{3,0,2,1:T(8,128)} %copy-done.8, f32[2,64,256,32]{2,3,1,0:T(8,128)S(1)} %fusion.114, f32[32,2,64,256]{3,0,2,1:T(8,128)} %copy-done.7, ...), kind=kOutput, calls=%fused_computation.32 | convolution fusion | flops 411056128 | bytes 33554432 | tf_op jit(solution)/shard_map/transpose(jvp(bkqc,pq->bkpc))/dot_general | solution.py:128
  986.3 38.2 %all-reduce.21 = (f32[2,3,256]{2,1,0:T(4,128)S(1)}, f32[2,3,3,256]{3,2,1,0:T(4,128)S(1)}, f32[2,3,256]{2,1,0:T(4,128)S(1)}, f32[2,256]{1,0:T(2,128)}, f32[2,1024]{1,0:T(2,128)}) all-reduce(f32[2,3,256]{2,1,0:T(4,128)S(1)} %pad_maximum_fusion.15, f32[2,3,3,256]{3,2,1,0:T(4,128)S(1)} %pad_maximum_fusion.12, ...), channel_id=1, replica_groups=mesh['dp'=8,'mp'=4] {'dp'}, use_global_device_ids=true, to_apply=%region_39.40 | all-reduce | flops 10240 | bytes 81920 | tf_op jit(solution)/shard_map/psum | solution.py:408
  1027.7 45.8 %all-reduce.27.cloned.1.call-done = (f32[2,1024]{1,0:T(2,128)}, f32[2,1024]{1,0:T(2,128)}, f32[2,33,64]{2,1,0:T(8,128)}, f32[2,64]{1,0:T(2,128)}, f32[2,64]{1,0:...) async-done(((f32[2,1024]{1,0:T(2,128)}, f32[2,1024]{1,0:T(2,128)}, ...) | async-done | bytes 100880 | tf_op jit(solution)/shard_map/psum | solution.py:413
  1074.9 73.6 %all-reduce.25.cloned.1.call-done = f32[2,64,256]{2,1,0:T(8,128)} async-done(((f32[2,64,256]{2,1,0:T(8,128)}), f32[2,64,256]{2,1,0:T(8,128)}) %all-reduce.25.cloned.1.call-update) | async-done | bytes 131088 | tf_op jit(solution)/shard_map/psum | solution.py:408
  1148.5 71.6 %reduce-scatter.31.cloned.1.call-done = f32[2,256,128]{2,1,0:T(8,128)} async-done(((f32[2,256,1024]{2,1,0:T(8,128)}), f32[2,256,128]{2,1,0:T(8,128)}) %reduce-scatter.31.cloned.1.call-update) | async-done | bytes 262160 | tf_op jit(solution)/shard_map/reduce_scatter | solution.py:404
  1220.1 152.5 %reduce-scatter.35.cloned.1.call-done = f32[2,1024,128]{2,1,0:T(8,128)} async-done(((f32[2,1024,1024]{2,1,0:T(8,128)}), f32[2,1024,128]{2,1,0:T(8,128)}) %reduce-scatter.35.cloned.1.call-update) | async-done | bytes 1048592 | tf_op jit(solution)/shard_map/reduce_scatter | solution.py:406
  1372.6 152.7 %reduce-scatter.33.cloned.1.call-done = f32[2,128,1024]{2,1,0:T(8,128)} async-done(((f32[2,1024,1024]{2,1,0:T(8,128)}), f32[2,128,1024]{2,1,0:T(8,128)}) %reduce-scatter.33.cloned.1.call-update) | async-done | bytes 1048592 | tf_op jit(solution)/shard_map/reduce_scatter | solution.py:405
  1525.3 121.6 %reduce-scatter.29.cloned.1.call-done = f32[2,128,3,256]{3,1,2,0:T(8,128)} async-done(((f32[2,1024,3,256]{3,1,2,0:T(8,128)}), f32[2,128,3,256]{3,1,2,0:T(8,128)}) %reduce-scatter.29.cloned.1.call-update) | async-done | bytes 786448 | tf_op jit(solution)/shard_map/reduce_scatter | solution.py:403
  (678 shorter events, 599.7 us)
Async XLA Ops:
  7.2 58.6 %all-gather.10.cloned.1.call-start = ((), (), s32[]{:S(2)}) async-start(), calls=%async_computation.12 | async-start | bytes 2621440 | tf_op jit(solution)/shard_map/all_gather | solution.py:199
  13.6 166.1 %reduce-scatter.13.cloned.1.call-start = ((), (), s32[]{:S(2)}) async-start(), calls=%async_computation.13 | async-start | bytes 2621440 | tf_op jit(solution)/shard_map/reduce_scatter | solution.py:203
  17.0 263.3 %copy-start.86 = (f32[1024]{0:T(1024)}, f32[1024]{0:T(1024)S(1)}, u32[]{:S(2)}) copy-start(f32[1024]{0:T(1024)S(1)} %get-tuple-element.283) | copy-start | bytes 12292
  145.4 61.9 %all-gather.12.cloned.1.call-start = ((), (), s32[]{:S(2)}) async-start(), calls=%async_computation.14 | async-start | bytes 2621440 | tf_op jit(solution)/shard_map/all_gather | solution.py:199
  184.6 65.3 %reduce-scatter.15.cloned.1.call-start = ((), (), s32[]{:S(2)}) async-start(), calls=%async_computation.15 | async-start | bytes 2621440 | tf_op jit(solution)/shard_map/reduce_scatter | solution.py:203
  184.7 267.3 %copy-start.158 = (f32[1,1024]{1,0:T(1,128)}, f32[1,1024]{1,0:T(1,128)S(1)}, u32[]{:S(2)}) copy-start(f32[1,1024]{1,0:T(1,128)S(1)} %get-tuple-element.263) | copy-start | bytes 12292
  218.3 58.2 %all-gather.14.cloned.1.call-start = ((), (), s32[]{:S(2)}) async-start(), calls=%async_computation.16 | async-start | bytes 2621440 | tf_op jit(solution)/shard_map/all_gather | solution.py:199
  253.7 133.9 %reduce-scatter.17.cloned.1.call-start = ((), (), s32[]{:S(2)}) async-start(), calls=%async_computation.17 | async-start | bytes 2621440 | tf_op jit(solution)/shard_map/reduce_scatter | solution.py:203
  356.0 57.6 %all-gather.16.cloned.1.call-start = ((), (), s32[]{:S(2)}) async-start(), calls=%async_computation.18 | async-start | bytes 2621440 | tf_op jit(solution)/shard_map/all_gather | solution.py:199
  390.9 47.0 %all-gather.24.cloned.1.call-start = ((), (), s32[]{:S(2)}) async-start(), calls=%async_computation.32 | async-start | bytes 2621440 | tf_op jit(solution)/shard_map/all_gather | solution.py:212
  391.7 91.9 %reduce-scatter.21.cloned.1.call-start = ((), (), s32[]{:S(2)}) async-start(), calls=%async_computation.20 | async-start | bytes 2621440 | tf_op jit(solution)/shard_map/reduce_scatter | solution.py:216
  451.9 65.4 %reduce-scatter.19.cloned.1.call-start = ((), (), s32[]{:S(2)}) async-start(), calls=%async_computation.19 | async-start | bytes 2621440 | tf_op jit(solution)/shard_map/reduce_scatter | solution.py:203
  459.1 86.1 %all-gather.18.cloned.1.call-start = ((), (), s32[]{:S(2)}) async-start(), calls=%async_computation.21 | async-start | bytes 2621440 | tf_op jit(solution)/shard_map/all_gather | solution.py:212
  522.4 160.2 %reduce-scatter.23.cloned.1.call-start = ((), (), s32[]{:S(2)}) async-start(), calls=%async_computation.22 | async-start | bytes 2621440 | tf_op jit(solution)/shard_map/reduce_scatter | solution.py:216
  650.9 60.8 %all-gather.20.cloned.1.call-start = ((), (), s32[]{:S(2)}) async-start(), calls=%async_computation.23 | async-start | bytes 2621440 | tf_op jit(solution)/shard_map/all_gather | solution.py:212
  689.0 68.4 %reduce-scatter.25.cloned.1.call-start = ((), (), s32[]{:S(2)}) async-start(), calls=%async_computation.24 | async-start | bytes 2621440 | tf_op jit(solution)/shard_map/reduce_scatter | solution.py:216
  725.9 60.5 %all-gather.22.cloned.1.call-start = ((), (), s32[]{:S(2)}) async-start(), calls=%async_computation.25 | async-start | bytes 2621440 | tf_op jit(solution)/shard_map/all_gather | solution.py:212
  763.6 175.5 %reduce-scatter.27.cloned.1.call-start = ((), (), s32[]{:S(2)}) async-start(), calls=%async_computation.26 | async-start | bytes 2621440 | tf_op jit(solution)/shard_map/reduce_scatter | solution.py:216
  900.7 172.8 %all-reduce.27.cloned.1.call-start = ((), (), s32[]{:S(2)}) async-start(), calls=%async_computation.33 | async-start | bytes 319488 | tf_op jit(solution)/shard_map/psum | solution.py:413
  943.5 205.0 %all-reduce.25.cloned.1.call-start = ((), (), s32[]{:S(2)}) async-start(), calls=%async_computation.28 | async-start | bytes 262144 | tf_op jit(solution)/shard_map/psum | solution.py:408
  944.3 275.9 %reduce-scatter.31.cloned.1.call-start = ((), (), s32[]{:S(2)}) async-start(), calls=%async_computation.29 | async-start | bytes 2359296 | tf_op jit(solution)/shard_map/reduce_scatter | solution.py:404
  949.8 422.8 %reduce-scatter.35.cloned.1.call-start = ((), (), s32[]{:S(2)}) async-start(), calls=%async_computation.31 | async-start | bytes 9437184 | tf_op jit(solution)/shard_map/reduce_scatter | solution.py:406
  963.2 562.0 %reduce-scatter.33.cloned.1.call-start = ((), (), s32[]{:S(2)}) async-start(), calls=%async_computation.30 | async-start | bytes 9437184 | tf_op jit(solution)/shard_map/reduce_scatter | solution.py:405
  975.0 671.9 %reduce-scatter.29.cloned.1.call-start = ((), (), s32[]{:S(2)}) async-start(), calls=%async_computation.27 | async-start | bytes 7077888 | tf_op jit(solution)/shard_map/reduce_scatter | solution.py:403
  (174 other events, 3040.5 us)
Sparse Core Ops, SparseCore 0:
  13.7 25.3 all-gather.9
  145.5 34.1 reduce-scatter.12
  184.7 22.5 all-gather.11
  218.4 31.4 reduce-scatter.14
  253.8 22.5 all-gather.13
  356.1 31.4 reduce-scatter.16
  391.0 22.5 all-gather.15
  415.3 22.5 all-gather.23
  452.1 31.4 reduce-scatter.20
  485.9 31.3 reduce-scatter.18
  522.5 22.5 all-gather.17
  651.0 31.4 reduce-scatter.22
  689.1 22.5 all-gather.19
  726.0 31.4 reduce-scatter.24
  763.8 22.5 all-gather.21
  900.8 31.4 reduce-scatter.26
  943.7 129.7 all-reduce.26
  1077.6 70.8 all-reduce.24
  1152.6 67.4 reduce-scatter.30
  1224.2 148.3 reduce-scatter.34
  1377.2 148.0 reduce-scatter.32
  1529.5 117.3 reduce-scatter.28
where the time goes:
time: 1680 us; the launch traced here: 1670 us
  waiting for transfers between devices  953 us (57%)
  matrix products  527 us (31%)
  other arithmetic  80 us (5%)
  local copies, waits for them, and re-layouts  51.6 us (3%)
  blocking collectives  38.2 us (2%)
  between operations  18 us (1%)
    reduce_scatter x1, waiting for transfers between devices, shards(): lax.psum_scatter(stacked(7), 'dp', scatter_dimension=1, tiled=True)  153 us
    reduce_scatter x1, waiting for transfers between devices, shards(): lax.psum_scatter(stacked(9), 'dp', scatter_dimension=2, tiled=True)  152 us
    reduce_scatter x4, waiting for transfers between devices, scatter_rows(): lax.psum_scatter(term_fn(jnp.int32(0), local_rows * lax.axis_size('mp'))....  129 us
    reduce_scatter x1, waiting for transfers between devices, shards(): lax.psum_scatter(stacked(0), 'dp', scatter_dimension=1, tiled=True)  122 us
    reduce_scatter x4, waiting for transfers between devices, scatter_grads(): lax.psum_scatter(term_fn(jnp.int32(0), local_rows * lax.axis_size('mp'))....  87.5 us
    psum x1, waiting for transfers between devices, shards(): lax.psum((stacked(1), stacked(2), stacked(3), stacked(4), stacked(5), sta...  73.6 us
    reduce_scatter x1, waiting for transfers between devices, shards(): lax.psum_scatter(stacked(6), 'dp', scatter_dimension=2, tiled=True)  71.6 us
    all_gather x4, waiting for transfers between devices, gather_grads(): return lax.all_gather(gradient_low, 'mp', axis=0, tiled=True)  67.1 us
  transfers between devices with their start and end apart: 22, of which 20 were waited for; matrix products, arithmetic and copies ran while one was open for 11% of the time, Pallas kernels for 0%

commit v1 on v0

v1 whole, which is shorter than its diff:
```python
import math

import jax
import jax.numpy as jnp
import ml_dtypes
import numpy as np
from jax import lax
from jax.sharding import PartitionSpec as P

D = 1024
POS = 33
REACH = 896
WAVES = 2 * REACH
SHORT = 3

f32 = jnp.float32
bf16 = jnp.bfloat16
highest = lax.Precision.HIGHEST
norm_eps = 1e-05
slow_rate = math.log(100.0) / 1.5
fast_rate = math.log(100.0) / 0.3
GELU_A = math.sqrt(2.0 / math.pi)
GELU_B = 0.044715


def wave_table(length):
    freq = 2 * np.arange(REACH, dtype=np.int64) + 1
    phase = (freq[:, None] * np.arange(length, dtype=np.int64)[None, :]) % (2 * WAVES)
    angle = phase.astype(np.float64) * (math.pi / WAVES)
    return np.concatenate([np.cos(angle), -np.sin(angle)], axis=0).astype(ml_dtypes.bfloat16)


def position_table(length, rows):
    places = jnp.arange(rows, dtype=jnp.int32).astype(f32)
    band_count = (POS - 1) // 2
    band_index = jnp.arange(band_count, dtype=jnp.int32).astype(f32)
    band_freq = 0.0001 + band_index * ((band_count - 1 - 0.0001) / (band_count - 1))
    phases = places[:, None] * band_freq[None, :] * (2.0 * math.pi / length)
    return jnp.concatenate(
        [places[:, None] / (length - 1), jnp.cos(phases), -jnp.sin(phases)], axis=1
    )


def decay_window(length, rows, chan_index):
    places = jnp.arange(rows, dtype=jnp.int32).astype(f32)
    decay_rates = slow_rate + (fast_rate - slow_rate) * chan_index / (D - 1)
    return jnp.exp(-(places[:, None] / (length - 1)) * decay_rates[None, :])


def make_taps(w_in, b_in, f_in, w_mid, b_mid, f_mid, w_out, pos_table):
    hidden = jnp.sin(f_in * (jnp.dot(pos_table, w_in, precision=highest) + b_in))
    hidden = jnp.sin(f_mid * (jnp.dot(hidden, w_mid, precision=highest) + b_mid))
    return jnp.dot(hidden, w_out, precision=highest)


def core_swap(x):
    size = lax.axis_size("mp")
    return lax.ppermute(x, "mp", [(i, i ^ 1) for i in range(size)])


def chip_swap(x):
    size = lax.axis_size("mp")
    return lax.ppermute(x, "mp", [(i, i ^ 2) for i in range(size)])


def dot(a, b):
    return jnp.dot(a, b, preferred_element_type=f32)


def dot_rows(a, b):
    return lax.dot_general(a, b, (((0,), (0,)), ((), ())), preferred_element_type=f32)


def dot_cols(a, b):
    return lax.dot_general(a, b, (((1,), (1,)), ((), ())), preferred_element_type=f32)


def norm_parts(values):
    center = values - jnp.mean(values, axis=-1, keepdims=True)
    spread = jnp.mean(center * center, axis=-1, keepdims=True)
    rstd = lax.rsqrt(spread + norm_eps)
    return center * rstd, rstd


def layer_norm(values, gain_row, shift_row):
    unit, _ = norm_parts(values)
    return unit * gain_row + shift_row


def norm_back(grad, values, gain_row):
    unit, rstd = norm_parts(values)
    scaled = grad * gain_row
    gain_grad = jnp.sum(grad * unit, axis=0) * 0.5
    shift_grad = jnp.sum(grad, axis=0) * 0.5
    into = rstd * (
        scaled
        - jnp.mean(scaled, axis=-1, keepdims=True)
        - unit * jnp.mean(scaled * unit, axis=-1, keepdims=True)
    )
    return into, gain_grad, shift_grad


def gelu(v):
    return 0.5 * v * (1.0 + jnp.tanh(GELU_A * (v + GELU_B * v * v * v)))


def gelu_slope(v):
    t = jnp.tanh(GELU_A * (v + GELU_B * v * v * v))
    return 0.5 * (1.0 + t) + 0.5 * v * (1.0 - t * t) * (GELU_A * (1.0 + 3.0 * GELU_B * v * v))


def reduce_scatter_rows(grad, axis):
    index = lax.axis_index("dp")
    whole = lax.axis_size("dp")
    left, step = whole, 1
    while left > 1:
        shape = grad.shape
        split = grad.reshape(shape[:axis] + (left // 2, 2) + shape[axis + 1 :])
        bit = (index // step) % 2
        kept = lax.dynamic_index_in_dim(split, bit, axis + 1, keepdims=False)
        sent = lax.dynamic_index_in_dim(split, 1 - bit, axis + 1, keepdims=False)
        got = lax.ppermute(sent, "dp", [(i, i ^ step) for i in range(whole)])
        grad = kept.astype(f32) + got.astype(f32)
        left, step = left // 2, step * 2
        if left > 1:
            grad = grad.astype(bf16)
    return jnp.squeeze(grad, axis)


def sum_over(values, axis_name):
    size, step = lax.axis_size(axis_name), 1
    while step < size:
        perm = [(i, i ^ step) for i in range(size)]
        got = [lax.ppermute(v, axis_name, perm) for v in values]
        values = [a + b for a, b in zip(values, got)]
        step *= 2
    return values


def shards(
    tokens,
    seg_lengths,
    cotangent,
    mixer_norm_gain,
    mixer_norm_bias,
    in_weight,
    in_bias,
    conv_weight,
    conv_bias,
    filter_in,
    filter_in_bias,
    filter_in_freq,
    filter_mid,
    filter_mid_bias,
    filter_mid_freq,
    filter_out,
    skip_bias,
    out_weight,
    out_bias,
    feed_norm_gain,
    feed_norm_bias,
    feed_up,
    feed_up_bias,
    feed_down,
    feed_down_bias,
):
    block = tokens.shape[1]
    length = block * lax.axis_size("mp")
    channels = in_weight.shape[3]
    layers = in_weight.shape[0]
    spot = lax.axis_index("mp")
    core, chip = spot % 2, spot // 2
    chan_index = (spot * channels + jnp.arange(channels, dtype=jnp.int32)).astype(f32)
    pos_table = position_table(length, REACH)
    window = decay_window(length, REACH, chan_index)
    table = wave_table(length)
    waves = jnp.asarray(table)
    waves_t = jnp.asarray(np.ascontiguousarray(table.T))
    taps_waves = jnp.asarray(np.ascontiguousarray(table[:, :REACH]))
    taps_waves_t = jnp.asarray(np.ascontiguousarray(table[:, :REACH].T))

    first = seg_lengths[0, 0]
    places = jnp.arange(length, dtype=jnp.int32)
    in_first = (places < first)[:, None]
    seg_offset = jnp.where(places < first, places, places - first)
    lag_kept = [(seg_offset >= lag).astype(f32)[:, None, None] for lag in range(SHORT)]

    def own_rows(mine):
        other = chip_swap(mine)
        return jnp.concatenate(
            [jnp.where(chip == 0, mine, other), jnp.where(chip == 0, other, mine)], axis=0
        )

    def in_order(own, got):
        a = own.reshape(2, block, -1)
        b = got.reshape(2, block, -1)
        lo = jnp.where(core == 0, a, b)
        hi = jnp.where(core == 0, b, a)
        return jnp.stack([lo, hi], axis=1).reshape(4 * block, -1)

    def core_part(rows, which):
        split = rows.reshape(2, 2, block, -1)
        return lax.dynamic_index_in_dim(split, which, 1, keepdims=False).reshape(2 * block, -1)

    def reduce_pair(keep, got):
        here = keep + got.astype(f32)
        there = chip_swap(here.astype(bf16))
        return here + there.astype(f32)

    def split_spectrum(spec):
        return spec[:REACH], spec[REACH:]

    def pieces_of(values):
        return jnp.concatenate(
            [jnp.where(in_first, values, 0.0), jnp.where(in_first, 0.0, values)], axis=1
        ).astype(bf16)

    def merge(pieces):
        return jnp.where(in_first, pieces[:, :channels], pieces[:, channels:])

    def twice(spec):
        return jnp.concatenate([spec, spec], axis=1)

    filt = []
    for layer in range(layers):
        taps, pull = jax.vjp(
            lambda *args: make_taps(*args, pos_table) * window,
            filter_in[layer],
            filter_in_bias[layer],
            filter_in_freq[layer],
            filter_mid[layer],
            filter_mid_bias[layer],
            filter_mid_freq[layer],
            filter_out[layer],
        )
        spec = dot(taps_waves, taps.astype(bf16)) * (2.0 / WAVES)
        filt.append((spec, pull))

    def short(proj, layer):
        total = conv_bias[layer] + proj * conv_weight[layer][:, 0]
        for lag in range(1, SHORT):
            moved = jnp.pad(proj[:-lag], ((lag, 0), (0, 0), (0, 0)))
            total = total + moved * conv_weight[layer][:, lag] * lag_kept[lag]
        return total

    residual = own_rows(tokens[0]).astype(f32)
    stored = []
    for layer in range(layers):
        entry = residual
        normed_own = layer_norm(
            residual, mixer_norm_gain[layer], mixer_norm_bias[layer]
        ).astype(bf16)
        normed = in_order(normed_own, core_swap(normed_own))
        proj = (
            dot(normed, in_weight[layer].reshape(D, -1)).reshape(length, 3, channels)
            + in_bias[layer]
        )
        shorted = short(proj, layer)
        gated = shorted[:, 2] * shorted[:, 1]
        gate_spec = dot(waves, pieces_of(gated))
        taps_re, taps_im = split_spectrum(twice(filt[layer][0]))
        gate_re, gate_im = split_spectrum(gate_spec)
        prod = jnp.concatenate(
            [gate_re * taps_re - gate_im * taps_im, gate_re * taps_im + gate_im * taps_re], axis=0
        ).astype(bf16)
        longc = merge(dot(waves_t, prod)) + skip_bias[layer] * gated
        mixed = (longc * shorted[:, 0]).astype(bf16)
        sent = dot(core_part(mixed, 1 - core), out_weight[layer]).astype(bf16)
        got = core_swap(sent)
        keep = dot(core_part(mixed, core), out_weight[layer])
        middle = residual + reduce_pair(keep, got) + out_bias[layer]
        feed_own = layer_norm(middle, feed_norm_gain[layer], feed_norm_bias[layer]).astype(bf16)
        feed_got = core_swap(feed_own)
        pre_own = dot(feed_own, feed_up[layer]) + feed_up_bias[layer]
        hid_own = gelu(pre_own).astype(bf16)
        pre_got = dot(feed_got, feed_up[layer]) + feed_up_bias[layer]
        hid_got = gelu(pre_got).astype(bf16)
        got = core_swap(dot(hid_got, feed_down[layer]).astype(bf16))
        keep = dot(hid_own, feed_down[layer])
        branch = reduce_pair(keep, got)
        stored.append(
            (
                entry,
                normed,
                proj,
                gate_spec.astype(bf16),
                longc,
                mixed,
                middle,
                feed_own,
                feed_got,
                pre_own,
                pre_got,
                hid_own,
                hid_got,
            )
        )
        residual = middle + branch + feed_down_bias[layer]
    outputs = lax.dynamic_slice_in_dim(residual, chip * block, block, 0)

    gradient = own_rows(cotangent[0]).astype(f32)
    big = [None] * layers
    small = [None] * layers
    shared = [None] * layers
    chunks = lax.axis_size("dp")

    def by_rows(grad):
        return reduce_scatter_rows(
            grad.astype(bf16).reshape(chunks, grad.shape[0] // chunks, grad.shape[1]), 0
        )

    def by_cols(grad):
        return reduce_scatter_rows(
            grad.astype(bf16).reshape(grad.shape[0], chunks, grad.shape[1] // chunks), 1
        )

    for layer in reversed(range(layers)):
        (
            entry,
            normed,
            proj,
            gate_spec,
            longc,
            mixed,
            middle,
            feed_own,
            feed_got,
            pre_own,
            pre_got,
            hid_own,
            hid_got,
        ) = stored[layer]
        down_bias_grad = jnp.sum(gradient, axis=0) * 0.5
        low_own = gradient.astype(bf16)
        low_got = core_swap(low_own)
        pg_own = dot_cols(low_own, feed_down[layer]) * gelu_slope(pre_own)
        up_own = pg_own.astype(bf16)
        pg_got = dot_cols(low_got, feed_down[layer]) * gelu_slope(pre_got)
        up_got = pg_got.astype(bf16)
        got = core_swap(dot_cols(up_got, feed_up[layer]).astype(bf16))
        keep = dot_cols(up_own, feed_up[layer])
        feed_grad = reduce_pair(keep, got)
        up_bias_grad = jnp.sum(pg_own, axis=0) + jnp.sum(pg_got, axis=0)
        down_grad = dot_rows(
            jnp.concatenate([hid_own, hid_got], axis=0), jnp.concatenate([low_own, low_got], axis=0)
        )
        up_grad = dot_rows(
            jnp.concatenate([feed_own, feed_got], axis=0), jnp.concatenate([up_own, up_got], axis=0)
        )
        down_big = by_cols(down_grad)
        up_big = by_rows(up_grad)
        into, feed_gain_grad, feed_shift_grad = norm_back(
            feed_grad, middle, feed_norm_gain[layer]
        )
        gradient = gradient + into
        out_bias_grad = jnp.sum(gradient, axis=0) * 0.5
        out_own = gradient.astype(bf16)
        out_low = in_order(out_own, core_swap(out_own))
        mixed_grad = dot_cols(out_low, out_weight[layer])
        out_big = by_cols(dot_rows(mixed, out_low))

        shorted = short(proj, layer)
        gated = shorted[:, 2] * shorted[:, 1]
        long_grad = mixed_grad * shorted[:, 0]
        first_grad = mixed_grad * longc
        skip_grad = jnp.sum(long_grad * gated, axis=0)
        long_spec = dot(waves, pieces_of(long_grad))
        taps_re, taps_im = split_spectrum(twice(filt[layer][0]))
        long_re, long_im = split_spectrum(long_spec)
        gate_re, gate_im = split_spectrum(gate_spec.astype(f32))
        prod = jnp.concatenate(
            [long_re * taps_re + long_im * taps_im, long_im * taps_re - long_re * taps_im], axis=0
        ).astype(bf16)
        gated_grad = merge(dot(waves_t, prod)) + skip_bias[layer] * long_grad
        corr_re = gate_re * long_re + gate_im * long_im
        corr_im = gate_re * long_im - gate_im * long_re
        corr = jnp.concatenate([corr_re, corr_im], axis=0)
        corr = (corr[:, :channels] + corr[:, channels:]).astype(bf16)
        taps_grad = dot(taps_waves_t, corr) * (2.0 / WAVES)
        filter_grads = filt[layer][1](taps_grad)
        short_grad = jnp.stack(
            [first_grad, gated_grad * shorted[:, 2], gated_grad * shorted[:, 1]], axis=1
        )
        conv_bias_grad = jnp.sum(short_grad, axis=0)
        proj_grad = short_grad * conv_weight[layer][:, 0]
        conv_grads = [jnp.sum(short_grad * proj, axis=0)]
        for lag in range(1, SHORT):
            kept = short_grad * lag_kept[lag]
            moved = jnp.pad(kept[lag:], ((0, lag), (0, 0), (0, 0)))
            proj_grad = proj_grad + moved * conv_weight[layer][:, lag]
            conv_grads.append(jnp.sum(moved * proj, axis=0))
        conv_weight_grad = jnp.stack(conv_grads, axis=1)
        in_bias_grad = jnp.sum(proj_grad, axis=0)
        in_low = proj_grad.astype(bf16).reshape(length, -1)
        flat_in = in_weight[layer].reshape(D, -1)
        in_big = by_rows(dot_rows(normed, in_low))
        got = core_swap(dot_cols(core_part(in_low, 1 - core), flat_in).astype(bf16))
        keep = dot_cols(core_part(in_low, core), flat_in)
        into, mixer_gain_grad, mixer_shift_grad = norm_back(
            reduce_pair(keep, got), entry, mixer_norm_gain[layer]
        )
        gradient = gradient + into

        big[layer] = (in_big.reshape(-1, 3, channels), out_big, up_big, down_big)
        small[layer] = jnp.concatenate(
            [
                in_bias_grad,
                conv_weight_grad.reshape(-1, channels),
                conv_bias_grad,
                filter_grads[6],
                skip_grad[None],
                up_bias_grad.reshape(-1, channels),
            ],
            axis=0,
        )
        shared[layer] = (
            jnp.stack(
                [
                    mixer_gain_grad,
                    mixer_shift_grad,
                    out_bias_grad,
                    feed_gain_grad,
                    feed_shift_grad,
                    down_bias_grad,
                ]
            ),
            jnp.concatenate(
                [
                    filter_grads[0],
                    filter_grads[1][None],
                    filter_grads[2][None],
                    filter_grads[3],
                    filter_grads[4][None],
                    filter_grads[5][None],
                ],
                axis=0,
            ),
        )
    token_grad = lax.dynamic_slice_in_dim(gradient, chip * block, block, 0)

    sums = []
    for layer in range(layers):
        by_chan, wide, narrow = sum_over([small[layer], *shared[layer]], "dp")
        wide, narrow = sum_over([wide, narrow], "mp")
        sums.append((by_chan, wide, narrow))

    def both(pick):
        return jnp.stack([pick(layer) for layer in range(layers)])

    def chan(lo, hi):
        return both(lambda layer: sums[layer][0][lo:hi])

    def wide(row):
        return both(lambda layer: sums[layer][1][row])

    def narrow(lo, hi):
        return both(lambda layer: sums[layer][2][lo:hi])

    filt_width = filter_mid.shape[1]
    at = np.cumsum([0, 3, 3 * SHORT, 3, filt_width, 1, feed_up.shape[2] // channels])
    return (
        outputs[None],
        token_grad[None],
        wide(0),
        wide(1),
        both(lambda layer: big[layer][0]),
        chan(at[0], at[1]),
        chan(at[1], at[2]).reshape(layers, 3, SHORT, channels),
        chan(at[2], at[3]),
        narrow(0, POS),
        narrow(POS, POS + 1)[:, 0],
        narrow(POS + 1, POS + 2)[:, 0],
        narrow(POS + 2, POS + 2 + filt_width),
        narrow(POS + 2 + filt_width, POS + 3 + filt_width)[:, 0],
        narrow(POS + 3 + filt_width, POS + 4 + filt_width)[:, 0],
        chan(at[3], at[4]),
        chan(at[4], at[5])[:, 0],
        both(lambda layer: big[layer][1]),
        wide(2),
        wide(3),
        wide(4),
        both(lambda layer: big[layer][2]),
        chan(at[5], at[6]).reshape(layers, -1),
        both(lambda layer: big[layer][3]),
        wide(5),
    )


def solution(mesh):
    in_specs = (
        P("dp", "mp", None),
        P("dp", None),
        P("dp", "mp", None),
        P(),
        P(),
        P(None, None, None, "mp"),
        P(None, None, "mp"),
        P(None, None, None, "mp"),
        P(None, None, "mp"),
        P(),
        P(),
        P(),
        P(),
        P(),
        P(),
        P(None, None, "mp"),
        P(None, "mp"),
        P(None, "mp", None),
        P(),
        P(),
        P(),
        P(None, None, "mp"),
        P(None, "mp"),
        P(None, "mp", None),
        P(),
    )
    out_specs = (
        P("dp", "mp", None),
        P("dp", "mp", None),
        P(),
        P(),
        P(None, "dp", None, "mp"),
        P(None, None, "mp"),
        P(None, None, None, "mp"),
        P(None, None, "mp"),
        P(),
        P(),
        P(),
        P(),
        P(),
        P(),
        P(None, None, "mp"),
        P(None, "mp"),
        P(None, "mp", "dp"),
        P(),
        P(),
        P(),
        P(None, "dp", "mp"),
        P(None, "mp"),
        P(None, "mp", "dp"),
        P(),
    )
    return jax.shard_map(shards, mesh=mesh, in_specs=in_specs, out_specs=out_specs, check_vma=False)
```

time: 1680 us -> 736 us (0.44)
  waiting for transfers between devices: 953 us -> 254 us
  matrix products: 527 us -> 153 us
  local copies, waits for them, and re-layouts: 51.6 us -> 134 us
  starting transfers between devices: 2.13 us -> 71.1 us
  blocking collectives: 38.2 us -> 0 us
  other arithmetic: 80 us -> 109 us
    reduce_scatter x12 -> x0, waiting for transfers between devices: 715 us -> none  [the longest x1 153 us: shards(): lax.psum_scatter(stacked(7), 'dp', scatter_dimension=1, tiled=True)]
    dot_general x112 -> x68, matrix products: 527 us -> 153 us  [the longest x30 61.9 us: dot(): return jnp.dot(a, b, preferred_element_type=f32)]
    ppermute x0 -> x76, waiting for transfers between devices: none -> 254 us  [the longest x10 120 us: chip_swap(): return lax.ppermute(x, 'mp', [(i, i ^ 2) for i in range(size)])]
    psum x2 -> x0, waiting for transfers between devices: 119 us -> none  [the longest x1 73.6 us: shards(): lax.psum((stacked(1), stacked(2), stacked(3), stacked(4), stacked(5), sta...]
    all_gather x8 -> x0, waiting for transfers between devices: 118 us -> none  [the longest x4 67.1 us: gather_grads(): return lax.all_gather(gradient_low, 'mp', axis=0, tiled=True)]
    ppermute x0 -> x76, starting transfers between devices: none -> 71.1 us  [the longest x24 30.6 us: reduce_scatter_rows(): got = lax.ppermute(sent, 'dp', [(i, i ^ step) for i in range(whole)])]
    psum x1 -> x0, blocking collectives: 38.2 us -> none  [shards(): lax.psum((stacked(1), stacked(2), stacked(3), stacked(4), stacked(5), sta...]
    dynamic_slice x0 -> x17, local copies, waits for them, and re-layouts: none -> 36.8 us  [the longest x8 25.6 us: core_part(): lax.dynamic_index_in_dim(split, which, 1, keepdims=False)]
  transfers between devices with their start and end apart: 22 -> 76, of which waited for: 20 -> 34; matrix products, arithmetic and copies ran while one was open for 11% -> 35% of each run, Pallas kernels for 0% -> 0%
where the time goes in v1:
time: 736 us; the launch traced here: 725 us
  waiting for transfers between devices  254 us (35%)
  matrix products  153 us (21%)
  local copies, waits for them, and re-layouts  134 us (18%)
  other arithmetic  109 us (15%)
  starting transfers between devices  71.1 us (10%)
    ppermute x10, waiting for transfers between devices, chip_swap(): return lax.ppermute(x, 'mp', [(i, i ^ 2) for i in range(size)])  120 us
    ppermute x24, waiting for transfers between devices, reduce_scatter_rows(): got = lax.ppermute(sent, 'dp', [(i, i ^ step) for i in range(whole)])  103 us
    dot_general x30, matrix products, dot(): return jnp.dot(a, b, preferred_element_type=f32)  61.9 us
    unnamed x511, local copies, waits for them, and re-layouts  48 us
    dot_general x14, matrix products, dot_cols(): lax.dot_general(a, b, (((1,), (1,)), ((), ())), preferred_element_type=f32)  43.7 us
    ppermute x24, starting transfers between devices, reduce_scatter_rows(): got = lax.ppermute(sent, 'dp', [(i, i ^ step) for i in range(whole)])  30.6 us
    ppermute x26, starting transfers between devices, sum_over(): got = [lax.ppermute(v, axis_name, perm) for v in values]  29.2 us
    dynamic_slice x8, local copies, waits for them, and re-layouts, core_part(): lax.dynamic_index_in_dim(split, which, 1, keepdims=False)  25.6 us
  transfers between devices with their start and end apart: 76, of which 34 were waited for; matrix products, arithmetic and copies ran while one was open for 35% of the time, Pallas kernels for 0%

profile of v1, /device:TPU:0, one launch (start us, length us, event | category | flops | bytes accessed | tf_op | source)
XLA Modules:
  0.0 725.4 jit_solution(16304763181320353786)
XLA Ops:
  64.2 23.8 %collective-permute-done.3 = bf16[512,1024]{1,0:T(8,128)(2,1)S(1)} collective-permute-done((bf16[512,1024]{1,0:T(8,128)(2,1)S(1)}, bf16[512,1024]{1,0:T(8,128)(2,1)S(1)}, u32[]{:S(2)}, u32[]{:S(2)}) %collective-permute-start.3) | collective-permute-done | bytes 1048608 | tf_op jit(solution)/shard_map/ppermute | solution.py:63
  103.5 24.5 %collective-permute-done.6 = bf16[512,1024]{1,0:T(8,128)(2,1)S(1)} collective-permute-done((bf16[512,1024]{1,0:T(8,128)(2,1)S(1)}, bf16[512,1024]{1,0:T(8,128)(2,1)S(1)}, u32[]{:S(2)}, u32[]{:S(2)}) %collective-permute-start.6) | collective-permute-done | bytes 1048608 | tf_op jit(solution)/shard_map/ppermute | solution.py:63
  164.5 25.1 %collective-permute-done.9 = bf16[512,1024]{1,0:T(8,128)(2,1)S(1)} collective-permute-done((bf16[512,1024]{1,0:T(8,128)(2,1)S(1)}, bf16[512,1024]{1,0:T(8,128)(2,1)S(1)}, u32[]{:S(2)}, u32[]{:S(2)}) %collective-permute-start.9) | collective-permute-done | bytes 1048608 | tf_op jit(solution)/shard_map/ppermute | solution.py:63
  194.6 12.4 %collective-permute-done.13 = bf16[256,1024]{1,0:T(8,128)(2,1)} collective-permute-done((bf16[256,1024]{1,0:T(8,128)(2,1)}, bf16[256,1024]{1,0:T(8,128)(2,1)}, u32[]{:S(2)}, u32[]{:S(2)}) %collective-permute-start.13) | collective-permute-done | bytes 524320 | tf_op jit(solution)/shard_map/ppermute | solution.py:63
  227.1 4.9 fusion.333
  246.7 5.1 collective-permute-done.73
  255.1 18.6 %collective-permute-done.67 = bf16[4,128,1024]{2,1,0:T(8,128)(2,1)} collective-permute-done((bf16[4,128,1024]{2,1,0:T(8,128)(2,1)}, bf16[4,128,1024]{2,1,0:T(8,128)(2,1)}, u32[]{:S(2)}, u32[]{:S(2)}) %collective-permute-start.67) | collective-permute-done | bytes 1048608 | tf_op jit(solution)/shard_map/ppermute | solution.py:122
  283.1 11.3 %collective-permute-done.68 = bf16[2,128,1024]{2,1,0:T(8,128)(2,1)S(1)} collective-permute-done((bf16[2,128,1024]{2,1,0:T(8,128)(2,1)S(1)}, bf16[2,128,1024]{2,1,0:T(8,128)(2,1)S(1)}, u32[]{:S(2)}, u32[]{:S(2)}) %collective-permute-start.68) | collective-permute-done | bytes 524320 | tf_op jit(solution)/shard_map/ppermute | solution.py:122
  299.1 8.9 %collective-permute-done.69 = bf16[1,128,1024]{2,1,0:T(8,128)(2,1)S(1)} collective-permute-done((bf16[1,128,1024]{2,1,0:T(8,128)(2,1)S(1)}, bf16[1,128,1024]{2,1,0:T(8,128)(2,1)S(1)}, u32[]{:S(2)}, u32[]{:S(2)}) %collective-permute-start.69) | collective-permute-done | bytes 262176 | tf_op jit(solution)/shard_map/ppermute | solution.py:122
  315.9 10.6 %collective-permute-done.12 = bf16[512,1024]{1,0:T(8,128)(2,1)S(1)} collective-permute-done((bf16[512,1024]{1,0:T(8,128)(2,1)S(1)}, bf16[512,1024]{1,0:T(8,128)(2,1)S(1)}, u32[]{:S(2)}, u32[]{:S(2)}) %collective-permute-start.12) | collective-permute-done | bytes 1048608 | tf_op jit(solution)/shard_map/ppermute | solution.py:63
  357.8 5.9 add_bitcast_fusion.1
  388.5 4.9 constant_dynamic-slice_fusion.18
  400.7 5.0 copy.236
  444.5 6.0 collective-permute-done.19
  499.1 11.9 %collective-permute-done.64 = bf16[4,128,1024]{2,1,0:T(8,128)(2,1)} collective-permute-done((bf16[4,128,1024]{2,1,0:T(8,128)(2,1)}, bf16[4,128,1024]{2,1,0:T(8,128)(2,1)}, u32[]{:S(2)}, u32[]{:S(2)}) %collective-permute-start.64) | collective-permute-done | bytes 1048608 | tf_op jit(solution)/shard_map/ppermute | solution.py:122
  513.4 19.4 %collective-permute-done.70 = bf16[1024,4,128]{2,0,1:T(8,128)(2,1)S(1)} collective-permute-done((bf16[1024,4,128]{2,0,1:T(8,128)(2,1)}, bf16[1024,4,128]{2,0,1:T(8,128)(2,1)S(1)}, u32[]{:S(2)}, u32[]{:S(2)}) %collective-permute-start.70) | collective-permute-done | bytes 1048608 | tf_op jit(solution)/shard_map/ppermute | solution.py:122
  539.5 12.7 %collective-permute-done.71 = bf16[1024,2,128]{2,0,1:T(8,128)(2,1)S(1)} collective-permute-done((bf16[1024,2,128]{2,0,1:T(8,128)(2,1)S(1)}, bf16[1024,2,128]{2,0,1:T(8,128)(2,1)S(1)}, u32[]{:S(2)}, u32[]{:S(2)}) %collective-permute-start.71) | collective-permute-done | bytes 524320 | tf_op jit(solution)/shard_map/ppermute | solution.py:122
  553.7 7.3 %collective-permute-done.22 = bf16[512,1024]{1,0:T(8,128)(2,1)S(1)} collective-permute-done((bf16[512,1024]{1,0:T(8,128)(2,1)S(1)}, bf16[512,1024]{1,0:T(8,128)(2,1)S(1)}, u32[]{:S(2)}, u32[]{:S(2)}) %collective-permute-start.22) | collective-permute-done | bytes 1048608 | tf_op jit(solution)/shard_map/ppermute | solution.py:63
  608.5 5.7 fusion.311
  633.3 4.8 copy.246
  667.1 4.9 collective-permute-done.59
  683.0 5.1 collective-permute-done.37
  688.6 10.8 %collective-permute-done.25 = bf16[512,1024]{1,0:T(8,128)(2,1)S(1)} collective-permute-done((bf16[512,1024]{1,0:T(8,128)(2,1)S(1)}, bf16[512,1024]{1,0:T(8,128)(2,1)S(1)}, u32[]{:S(2)}, u32[]{:S(2)}) %collective-permute-start.25) | collective-permute-done | bytes 1048608 | tf_op jit(solution)/shard_map/ppermute | solution.py:63
  711.1 4.8 collective-permute-done.28
  (991 shorter events, 466.2 us)
Async XLA Ops:
  0.7 31.9 %collective-permute-start = (bf16[256,1024]{1,0:T(8,128)(2,1)}, bf16[256,1024]{1,0:T(8,128)(2,1)}, u32[]{:S(2)}, u32[]{:S(2)}) collective-permute-start(bf16[256,1024]{1,0:T(8,128)(2,1)} %bitcast.657), channel_id=1, source_target_pairs={{0,2},{1,3},{2,0},{3,1},{4,6},{5,7},{6,4},{7,5},{8,10},{9,11},{10,... | collective-permute-start | bytes 1572872 | tf_op jit(solution)/shard_map/ppermute | solution.py:63
  62.8 25.3 %collective-permute-start.3 = (bf16[512,1024]{1,0:T(8,128)(2,1)S(1)}, bf16[512,1024]{1,0:T(8,128)(2,1)S(1)}, u32[]{:S(2)}, u32[]{:S(2)}) collective-permute-start(bf16[512,1024]{1,0:T(8,128)(2,1)S(1)} %get-tuple-element.313), channel_id=1, source_target_pairs={{0,2},{1,3},{2,0},{3,1},{4,6},{5,7},{6,4},{7,5},{8,10},{9,11},{10,... | collective-permute-start | bytes 3145736 | tf_op jit(solution)/shard_map/ppermute | solution.py:63
  102.8 25.3 %collective-permute-start.6 = (bf16[512,1024]{1,0:T(8,128)(2,1)S(1)}, bf16[512,1024]{1,0:T(8,128)(2,1)S(1)}, u32[]{:S(2)}, u32[]{:S(2)}) collective-permute-start(bf16[512,1024]{1,0:T(8,128)(2,1)S(1)} %get-tuple-element.316), channel_id=1, source_target_pairs={{0,2},{1,3},{2,0},{3,1},{4,6},{5,7},{6,4},{7,5},{8,10},{9,11},{10,... | collective-permute-start | bytes 3145736 | tf_op jit(solution)/shard_map/ppermute | solution.py:63
  164.2 25.5 %collective-permute-start.9 = (bf16[512,1024]{1,0:T(8,128)(2,1)S(1)}, bf16[512,1024]{1,0:T(8,128)(2,1)S(1)}, u32[]{:S(2)}, u32[]{:S(2)}) collective-permute-start(bf16[512,1024]{1,0:T(8,128)(2,1)S(1)} %get-tuple-element.318), channel_id=1, source_target_pairs={{0,2},{1,3},{2,0},{3,1},{4,6},{5,7},{6,4},{7,5},{8,10},{9,11},{10,... | collective-permute-start | bytes 3145736 | tf_op jit(solution)/shard_map/ppermute | solution.py:63
  225.6 26.3 %collective-permute-start.73 = (bf16[1024,4,128]{2,0,1:T(8,128)(2,1)}, bf16[1024,4,128]{2,0,1:T(8,128)(2,1)}, u32[]{:S(2)}, u32[]{:S(2)}) collective-permute-start(bf16[1024,4,128]{2,0,1:T(8,128)(2,1)} %bitcast.650), channel_id=1, source_target_pairs={{0,4},{4,0},{8,12},{12,8},{16,20},{20,16},{24,28},{28,24},{1,5},{5... | collective-permute-start | bytes 3145736 | tf_op jit(solution)/shard_map/ppermute | solution.py:122
  237.2 36.5 %collective-permute-start.67 = (bf16[4,128,1024]{2,1,0:T(8,128)(2,1)}, bf16[4,128,1024]{2,1,0:T(8,128)(2,1)}, u32[]{:S(2)}, u32[]{:S(2)}) collective-permute-start(bf16[4,128,1024]{2,1,0:T(8,128)(2,1)} %dynamic-slice_bitcast_fusion), channel_id=1, source_target_pairs={{0,4},{4,0},{8,12},{12,8},{16,20},{20,16},{24,28},{28,24},{1,5},{5... | collective-permute-start | bytes 3145736 | tf_op jit(solution)/shard_map/ppermute | solution.py:122
  240.0 37.0 %collective-permute-start.15 = (bf16[512,1024]{1,0:T(8,128)(2,1)}, bf16[512,1024]{1,0:T(8,128)(2,1)}, u32[]{:S(2)}, u32[]{:S(2)}) collective-permute-start(bf16[512,1024]{1,0:T(8,128)(2,1)} %fusion.134), channel_id=1, source_target_pairs={{0,1},{1,0},{2,3},{3,2},{4,5},{5,4},{6,7},{7,6},{8,9},{9,8},{10,11... | collective-permute-start | bytes 3145736 | tf_op jit(solution)/shard_map/ppermute | solution.py:58
  246.2 50.2 %collective-permute-start.11 = (bf16[512,1024]{1,0:T(8,128)(2,1)S(1)}, bf16[512,1024]{1,0:T(8,128)(2,1)S(1)}, u32[]{:S(2)}, u32[]{:S(2)}) collective-permute-start(bf16[512,1024]{1,0:T(8,128)(2,1)S(1)} %fusion.137), channel_id=1, source_target_pairs={{0,1},{1,0},{2,3},{3,2},{4,5},{5,4},{6,7},{7,6},{8,9},{9,8},{10,11... | collective-permute-start | bytes 3145736 | tf_op jit(solution)/shard_map/ppermute | solution.py:58
  253.4 26.8 %collective-permute-start.74 = (bf16[1024,2,128]{2,0,1:T(8,128)(2,1)S(1)}, bf16[1024,2,128]{2,0,1:T(8,128)(2,1)S(1)}, u32[]{:S(2)}, u32[]{:S(2)}) collective-permute-start(bf16[1024,2,128]{2,0,1:T(8,128)(2,1)S(1)} %dynamic-slice_bitcast_fusion.4), channel_id=1, source_target_pairs={{0,8},{4,12},{8,0},{12,4},{16,24},{20,28},{24,16},{28,20},{1,9},{5... | collective-permute-start | bytes 1572872 | tf_op jit(solution)/shard_map/ppermute | solution.py:122
  279.7 29.2 %collective-permute-start.16 = (bf16[512,1024]{1,0:T(8,128)(2,1)S(1)}, bf16[512,1024]{1,0:T(8,128)(2,1)S(1)}, u32[]{:S(2)}, u32[]{:S(2)}) collective-permute-start(bf16[512,1024]{1,0:T(8,128)(2,1)S(1)} %get-tuple-element.322), channel_id=1, source_target_pairs={{0,2},{1,3},{2,0},{3,1},{4,6},{5,7},{6,4},{7,5},{8,10},{9,11},{10,... | collective-permute-start | bytes 3145736 | tf_op jit(solution)/shard_map/ppermute | solution.py:63
  297.7 28.8 %collective-permute-start.12 = (bf16[512,1024]{1,0:T(8,128)(2,1)S(1)}, bf16[512,1024]{1,0:T(8,128)(2,1)S(1)}, u32[]{:S(2)}, u32[]{:S(2)}) collective-permute-start(bf16[512,1024]{1,0:T(8,128)(2,1)S(1)} %get-tuple-element.327), channel_id=1, source_target_pairs={{0,2},{1,3},{2,0},{3,1},{4,6},{5,7},{6,4},{7,5},{8,10},{9,11},{10,... | collective-permute-start | bytes 3145736 | tf_op jit(solution)/shard_map/ppermute | solution.py:63
  354.7 64.6 %collective-permute-start.61 = (bf16[256,4,128]{2,0,1:T(8,128)(2,1)}, bf16[256,4,128]{2,0,1:T(8,128)(2,1)}, u32[]{:S(2)}, u32[]{:S(2)}) collective-permute-start(bf16[256,4,128]{2,0,1:T(8,128)(2,1)} %bitcast.579), channel_id=1, source_target_pairs={{0,4},{4,0},{8,12},{12,8},{16,20},{20,16},{24,28},{28,24},{1,5},{5... | collective-permute-start | bytes 786440 | tf_op jit(solution)/shard_map/ppermute | solution.py:122
  371.4 34.6 %collective-permute-start.45 = (f32[84,256]{1,0:T(8,128)S(1)}, f32[84,256]{1,0:T(8,128)S(1)}, u32[]{:S(2)}, u32[]{:S(2)}) collective-permute-start(f32[84,256]{1,0:T(8,128)S(1)} %concatenate.110), channel_id=1, source_target_pairs={{0,4},{4,0},{8,12},{12,8},{16,20},{20,16},{24,28},{28,24},{1,5},{5... | collective-permute-start | bytes 258056 | tf_op jit(solution)/shard_map/ppermute | solution.py:134
  387.2 34.7 %collective-permute-start.39 = (bf16[4,128,768]{2,1,0:T(8,128)(2,1)}, bf16[4,128,768]{2,1,0:T(8,128)(2,1)}, u32[]{:S(2)}, u32[]{:S(2)}) collective-permute-start(bf16[4,128,768]{2,1,0:T(8,128)(2,1)} %dynamic-slice_bitcast_fusion.2), channel_id=1, source_target_pairs={{0,4},{4,0},{8,12},{12,8},{16,20},{20,16},{24,28},{28,24},{1,5},{5... | collective-permute-start | bytes 2359304 | tf_op jit(solution)/shard_map/ppermute | solution.py:122
  425.8 24.7 %collective-permute-start.19 = (bf16[512,1024]{1,0:T(8,128)(2,1)}, bf16[512,1024]{1,0:T(8,128)(2,1)}, u32[]{:S(2)}, u32[]{:S(2)}) collective-permute-start(bf16[512,1024]{1,0:T(8,128)(2,1)} %get-tuple-element.324), channel_id=1, source_target_pairs={{0,2},{1,3},{2,0},{3,1},{4,6},{5,7},{6,4},{7,5},{8,10},{9,11},{10,... | collective-permute-start | bytes 3145736 | tf_op jit(solution)/shard_map/ppermute | solution.py:63
  433.4 28.0 %collective-permute-start.63 = (bf16[256,1,128]{2,0,1:T(8,128)(2,1)}, bf16[256,1,128]{2,0,1:T(8,128)(2,1)}, u32[]{:S(2)}, u32[]{:S(2)}) collective-permute-start(bf16[256,1,128]{2,0,1:T(8,128)(2,1)} %constant_dynamic-slice_fusion.8), channel_id=1, source_target_pairs={{0,16},{4,20},{8,24},{12,28},{16,0},{20,4},{24,8},{28,12},{1,17},{... | collective-permute-start | bytes 196616 | tf_op jit(solution)/shard_map/ppermute | solution.py:122
  441.8 26.5 %collective-permute-start.41 = (bf16[1,128,768]{2,1,0:T(8,128)(2,1)}, bf16[1,128,768]{2,1,0:T(8,128)(2,1)}, u32[]{:S(2)}, u32[]{:S(2)}) collective-permute-start(bf16[1,128,768]{2,1,0:T(8,128)(2,1)} %constant_dynamic-slice_fusion.14), channel_id=1, source_target_pairs={{0,16},{4,20},{8,24},{12,28},{16,0},{20,4},{24,8},{28,12},{1,17},{... | collective-permute-start | bytes 589832 | tf_op jit(solution)/shard_map/ppermute | solution.py:122
  484.8 26.3 %collective-permute-start.64 = (bf16[4,128,1024]{2,1,0:T(8,128)(2,1)}, bf16[4,128,1024]{2,1,0:T(8,128)(2,1)}, u32[]{:S(2)}, u32[]{:S(2)}) collective-permute-start(bf16[4,128,1024]{2,1,0:T(8,128)(2,1)} %dynamic-slice_bitcast_fusion.1), channel_id=1, source_target_pairs={{0,4},{4,0},{8,12},{12,8},{16,20},{20,16},{24,28},{28,24},{1,5},{5... | collective-permute-start | bytes 3145736 | tf_op jit(solution)/shard_map/ppermute | solution.py:122
  491.4 41.4 %collective-permute-start.70 = (bf16[1024,4,128]{2,0,1:T(8,128)(2,1)}, bf16[1024,4,128]{2,0,1:T(8,128)(2,1)S(1)}, u32[]{:S(2)}, u32[]{:S(2)}) collective-permute-start(bf16[1024,4,128]{2,0,1:T(8,128)(2,1)} %bitcast.649), channel_id=1, source_target_pairs={{0,4},{4,0},{8,12},{12,8},{16,20},{20,16},{24,28},{28,24},{1,5},{5... | collective-permute-start | bytes 3145736 | tf_op jit(solution)/shard_map/ppermute | solution.py:122
  497.2 36.6 %collective-permute-start.21 = (bf16[512,1024]{1,0:T(8,128)(2,1)}, bf16[512,1024]{1,0:T(8,128)(2,1)}, u32[]{:S(2)}, u32[]{:S(2)}) collective-permute-start(bf16[512,1024]{1,0:T(8,128)(2,1)} %fusion.128), channel_id=1, source_target_pairs={{0,1},{1,0},{2,3},{3,2},{4,5},{5,4},{6,7},{7,6},{8,9},{9,8},{10,11... | collective-permute-start | bytes 3145736 | tf_op jit(solution)/shard_map/ppermute | solution.py:58
  602.1 63.7 %collective-permute-start.58 = (bf16[256,4,128]{2,0,1:T(8,128)(2,1)}, bf16[256,4,128]{2,0,1:T(8,128)(2,1)}, u32[]{:S(2)}, u32[]{:S(2)}) collective-permute-start(bf16[256,4,128]{2,0,1:T(8,128)(2,1)} %bitcast.580), channel_id=1, source_target_pairs={{0,4},{4,0},{8,12},{12,8},{16,20},{20,16},{24,28},{28,24},{1,5},{5... | collective-permute-start | bytes 786440 | tf_op jit(solution)/shard_map/ppermute | solution.py:122
  614.5 30.5 %collective-permute-start.42 = (f32[84,256]{1,0:T(8,128)S(1)}, f32[84,256]{1,0:T(8,128)}, u32[]{:S(2)}, u32[]{:S(2)}) collective-permute-start(f32[84,256]{1,0:T(8,128)S(1)} %concatenate.108), channel_id=1, source_target_pairs={{0,4},{4,0},{8,12},{12,8},{16,20},{20,16},{24,28},{28,24},{1,5},{5... | collective-permute-start | bytes 258056 | tf_op jit(solution)/shard_map/ppermute | solution.py:134
  627.2 49.5 %collective-permute-start.36 = (bf16[4,128,768]{2,1,0:T(8,128)(2,1)}, bf16[4,128,768]{2,1,0:T(8,128)(2,1)}, u32[]{:S(2)}, u32[]{:S(2)}) collective-permute-start(bf16[4,128,768]{2,1,0:T(8,128)(2,1)} %dynamic-slice_bitcast_fusion.3), channel_id=1, source_target_pairs={{0,4},{4,0},{8,12},{12,8},{16,20},{20,16},{24,28},{28,24},{1,5},{5... | collective-permute-start | bytes 2359304 | tf_op jit(solution)/shard_map/ppermute | solution.py:122
  644.8 29.3 %collective-permute-start.24 = (bf16[512,1024]{1,0:T(8,128)(2,1)}, bf16[512,1024]{1,0:T(8,128)(2,1)S(1)}, u32[]{:S(2)}, u32[]{:S(2)}) collective-permute-start(bf16[512,1024]{1,0:T(8,128)(2,1)} %convolution_convert_fusion.2), channel_id=1, source_target_pairs={{0,1},{1,0},{2,3},{3,2},{4,5},{5,4},{6,7},{7,6},{8,9},{9,8},{10,11... | collective-permute-start | bytes 3145736 | tf_op jit(solution)/shard_map/ppermute | solution.py:58
  (295 other events, 3465.1 us)
